TPU v7x, 32 devices: a whole 2x2x4 slice. The times are simulated.
32 devices in a mesh: pipe: 2 (over y), dp: 4 (over z), tensor: 4 (over x, core).
Axes of the slice: x: 2, y: 2, z: 4, core: 2. Of those that a mesh axis runs over, the one named last changes fastest.
Arguments:
- tokens: bfloat16 [3072, 8192], P(('pipe', 'dp'), 'tensor'), parts along dimension 0, may hold values from -6 to 6
- pattern: int32 [128, 6], P('pipe'), parts along dimension 0, may hold values from 0 to 31, as said below
- blocks: bfloat16 [128, 6, 256, 256], P(('pipe', 'tensor'), None, 'dp'), parts along dimension 0, may hold values from -0.15625 to 0.15625
- left_factor: bfloat16 [16384, 512], P(('pipe', 'tensor'), 'dp'), parts along dimension 0, may hold values from -0.0625 to 0.0625
- right_factor: bfloat16 [1024, 16384], P(('pipe', 'dp'), 'tensor'), parts along dimension 0, may hold values from -0.25 to 0.25
- cotangent: bfloat16 [3072, 16384], P(('pipe', 'dp'), 'tensor'), parts along dimension 0, may hold values from -6 to 6
Outputs:
- hidden: bfloat16 [3072, 16384], P(('pipe', 'dp'), 'tensor'), parts along dimension 0
- token_grad: float32 [3072, 8192], P(('pipe', 'dp'), 'tensor'), parts along dimension 0
- block_grad: float32 [128, 6, 256, 256], P(('pipe', 'tensor'), None, 'dp'), parts along dimension 0
- left_grad: float32 [16384, 512], P(('pipe', 'tensor'), 'dp'), parts along dimension 0
- right_grad: float32 [1024, 16384], P(('pipe', 'dp'), 'tensor'), parts along dimension 0
There are 2 independent parts, one for each index of `pipe`. A program takes and returns all parts, laid end to end along the dimension named above; each array names one. Nothing has to cross between parts.
Inputs may be any that keep to these rules, and one draw needn't show every extreme that they name: `pattern`: row j lists the 6 input blocks feeding hidden block j: under a relabeling of the 32 input blocks drawn from the seed, they are the labels of (j mod 32) XOR s for s = 0 and then the powers of two below 32 in rising order; a row's entries are distinct.
All inputs are finite; a program needn't handle non-finite values.
Results may differ from a plain program's by a relative error of at most 0.017.
Values may be sent and summed in bfloat16 or wider, within the bound.
A program may use at most 256 MiB of HBM per device.

v0:
```python
import jax
import jax.numpy as jnp
from jax import lax
from jax.sharding import PartitionSpec as P

SQRT_HALF = 0.7071067811865476
INV_ROOT_TWO_PI = 0.3989422804014327


def gelu_parts(preact):
    normal_cdf = 0.5 * (1.0 + jax.scipy.special.erf(preact * SQRT_HALF))
    return (
        preact * normal_cdf,
        normal_cdf + preact * jnp.exp(-0.5 * preact * preact) * INV_ROOT_TWO_PI,
    )


def per_device(tokens, pattern, blocks, left_factor, right_factor, cotangent):
    tok_rows = tokens.shape[0]
    block_size = blocks.shape[3]
    local_cols = blocks.shape[0]
    slot_count = blocks.shape[1]
    full_tokens = lax.all_gather(tokens, "tensor", axis=1, tiled=True)
    block_count = full_tokens.shape[1] // block_size
    tensor_rank = lax.axis_index("tensor")
    local_pattern = lax.dynamic_slice_in_dim(pattern, tensor_rank * local_cols, local_cols, 0)
    picked = jnp.take(full_tokens.reshape(tok_rows, block_count, block_size), local_pattern, axis=1)
    inputs = picked
    butterfly = jnp.einsum(
        "tjkc,jkcd->tjd",
        inputs,
        lax.all_gather(blocks, "dp", axis=2, tiled=True),
        preferred_element_type=jnp.float32,
    )
    left_rows = lax.all_gather(left_factor, "dp", axis=1, tiled=True)
    whole_left = lax.all_gather(left_rows, "tensor", axis=0, tiled=True)
    rank_acts = jnp.dot(full_tokens, whole_left, preferred_element_type=jnp.float32).astype(
        jnp.bfloat16
    )
    inputs = rank_acts
    rank_part = jnp.dot(
        inputs,
        lax.all_gather(right_factor, "dp", axis=0, tiled=True),
        preferred_element_type=jnp.float32,
    )
    preact = butterfly.reshape(tok_rows, -1) + rank_part
    activated, slope_values = gelu_parts(preact)
    hidden = activated.astype(jnp.bfloat16)
    grad_pre = (cotangent.astype(jnp.float32) * slope_values).astype(jnp.bfloat16)
    rank_terms = lax.dot_general(
        grad_pre,
        lax.all_gather(right_factor, "dp", axis=0, tiled=True),
        (((1,), (1,)), ((), ())),
        preferred_element_type=jnp.float32,
    )
    rank_grad = lax.psum(rank_terms.astype(jnp.bfloat16), "tensor")
    right_term = lax.dot_general(
        rank_acts, grad_pre, (((0,), (0,)), ((), ())), preferred_element_type=jnp.float32
    )
    right_grad = lax.psum_scatter(
        right_term.astype(jnp.bfloat16), "dp", scatter_dimension=0, tiled=True
    ).astype(jnp.float32)
    left_term = lax.dot_general(
        tokens, rank_grad, (((0,), (0,)), ((), ())), preferred_element_type=jnp.float32
    )
    left_grad = lax.psum_scatter(
        left_term.astype(jnp.bfloat16), "dp", scatter_dimension=1, tiled=True
    ).astype(jnp.float32)
    grad_blocks = grad_pre.reshape(tok_rows, local_cols, block_size)
    block_term = jnp.einsum(
        "tjkc,tjd->jkcd", picked, grad_blocks, preferred_element_type=jnp.float32
    )
    block_grad = lax.psum_scatter(
        block_term.astype(jnp.bfloat16), "dp", scatter_dimension=2, tiled=True
    ).astype(jnp.float32)
    spread = jnp.einsum(
        "tjd,jkcd->tjkc",
        grad_blocks,
        lax.all_gather(blocks, "dp", axis=2, tiled=True),
        preferred_element_type=jnp.float32,
    )
    placed = (
        jnp.zeros((tok_rows, block_count, block_size), jnp.float32)
        .at[:, local_pattern.reshape(-1)]
        .add(spread.reshape(tok_rows, local_cols * slot_count, block_size))
    )
    token_part = lax.psum_scatter(
        placed.reshape(tok_rows, -1).astype(jnp.bfloat16), "tensor", scatter_dimension=1, tiled=True
    ).astype(jnp.float32)
    token_grad = token_part + lax.dot_general(
        rank_grad, left_rows, (((1,), (1,)), ((), ())), preferred_element_type=jnp.float32
    )
    return (hidden, token_grad, block_grad, left_grad, right_grad)


def solution(mesh):
    placed = (
        P(("pipe", "dp"), "tensor"),
        P("pipe", None),
        P(("pipe", "tensor"), None, "dp", None),
        P(("pipe", "tensor"), "dp"),
        P(("pipe", "dp"), "tensor"),
        P(("pipe", "dp"), "tensor"),
    )
    return jax.shard_map(
        per_device,
        mesh=mesh,
        in_specs=placed,
        out_specs=(
            P(("pipe", "dp"), "tensor"),
            P(("pipe", "dp"), "tensor"),
            P(("pipe", "tensor"), None, "dp", None),
            P(("pipe", "tensor"), "dp"),
            P(("pipe", "dp"), "tensor"),
        ),
        check_vma=False,
    )
```

profile of v0, /device:TPU:0, one launch (start us, length us, event | category | flops | bytes accessed | tf_op | source)
XLA Modules:
  0.0 936.8 jit_solution(5141369474184893608)
XLA Ops:
  7.2 0.0 copy-start.5
  7.2 0.0 all-gather.10.cloned.1.call-start
  7.2 0.7 all-gather.10.cloned.1.call-update
  7.9 0.0 all-gather.6.cloned.1.call-start
  8.0 2.6 copy.32
  10.5 0.0 all-gather.6.cloned.1.call-update
  10.6 0.0 all-gather.12.cloned.1.call-start
  10.6 47.9 %all-gather.10.cloned.1.call-done = bf16[2048,512]{1,0:T(8,128)(2,1)} async-done(((bf16[2048,128]{1,0:T(8,128)(2,1)}), bf16[2048,512]{1,0:T(8,128)(2,1)}) %all-gather.10.cloned.1.call-update) | async-done | bytes 2097168 | tf_op jit(solution)/shard_map/all_gather | solution.py:35
  58.5 0.0 all-gather.12.cloned.1.call-update
  58.6 0.0 all-gather.8.cloned.1.call-start
  58.6 0.5 all-gather.8.cloned.1.call-update
  59.1 0.0 all-gather.14.cloned.1.call-start
  59.2 0.5 all-gather.14.cloned.1.call-update
  59.7 0.0 all-reduce.2.cloned.1.call-start
  59.8 0.0 copy-done.5
  59.8 0.1 compare_and_fusion
  59.9 0.1 copy.31
  60.0 0.1 copy.33
  60.1 0.1 reshape.67
  60.2 45.2 %all-gather.6.cloned.1.call-done = bf16[384,8192]{0,1:T(8,128)(2,1)} async-done(((bf16[384,2048]{0,1:T(8,128)(2,1)}), bf16[384,8192]{0,1:T(8,128)(2,1)}) %all-gather.6.cloned.1.call-update) | async-done | bytes 6291472 | tf_op jit(solution)/shard_map/all_gather | solution.py:23
  105.3 8.6 copy.34
  114.0 13.0 %gather_fusion = bf16[96,384,256]{2,1,0:T(8,128)(2,1)} fusion(bf16[384,32,256]{2,0,1:T(8,128)(2,1)} %copy.34, s32[1024]{0:T(1024)S(1)} %pad_clamp_fusion), kind=kCustom, calls=%fused_computation | custom fusion | bytes 37749120 | tf_op jit(solution)/shard_map/jit(_take)/gather | solution.py:27
  126.9 24.7 %copy.35 = bf16[16,6,384,256]{2,3,1,0:T(8,128)(2,1)} copy(bf16[16,6,384,256]{3,2,1,0:T(8,128)(2,1)} %bitcast.47) | data formatting | bytes 37748736 | tf_op jit(solution)/shard_map/jit(_take)/gather | solution.py:27
  151.6 13.6 %all-gather.12.cloned.1.call-done = bf16[8192,512]{1,0:T(8,128)(2,1)} async-done(((bf16[2048,512]{1,0:T(8,128)(2,1)}), bf16[8192,512]{1,0:T(8,128)(2,1)}) %all-gather.12.cloned.1.call-update) | async-done | bytes 8388624 | tf_op jit(solution)/shard_map/all_gather | solution.py:36
  165.2 8.6 convolution_convert_fusion.3
  173.8 211.0 %all-gather.8.cloned.1.call-done = bf16[16,6,256,256]{3,2,1,0:T(8,128)(2,1)} async-done(((bf16[16,6,64,256]{3,2,1,0:T(8,128)(2,1)}), bf16[16,6,256,256]{3,2,1,0:T(8,128)(2,1)}) %all-gather.8.cloned.1.call-update) | async-done | bytes 12582928 | tf_op jit(solution)/shard_map/all_gather | solution.py:32
  384.9 16.6 %fusion.2 = f32[16,384,256,1]{1,2,3,0:T(8,128)} fusion(bf16[16,6,256,256]{3,2,1,0:T(8,128)(2,1)} %all-gather.8.cloned.1.call-done, bf16[16,6,384,256]{2,3,1,0:T(8,128)(2,1)} %copy.35, pred[16,6]{1,0:T(8,128)(4,1)S(1)} %copy.31), kind=kOutput, calls=%fused_computation.4 | convolution fusion | flops 4841275392 | bytes 37748832 | tf_op jit(solution)/shard_map/tjkc,jkcd->tjd/dot_general | solution.py:29
  401.5 6.6 copy.37
  408.1 57.2 %all-gather.14.cloned.1.call-done = bf16[512,4096]{1,0:T(8,128)(2,1)} async-done(((bf16[128,4096]{1,0:T(8,128)(2,1)}), bf16[512,4096]{1,0:T(8,128)(2,1)}) %all-gather.14.cloned.1.call-update) | async-done | bytes 4194320 | tf_op jit(solution)/shard_map/all_gather | solution.py:43
  465.3 10.5 %fusion.14 = (bf16[384,4096]{1,0:T(8,128)(2,1)S(1)}, bf16[384,4096]{1,0:T(8,128)(2,1)}) fusion(bf16[384,4096]{1,0:T(8,128)(2,1)} %param.11, f32[384,4096]{1,0:T(8,128)} %copy.37, bf16[384,512]{1,0:T(8,128)(2,1)S(1)} %convolution_convert_fusion.3, bf16[512,4096]{1,0:T(8,128)(2,1)} %all-gather.14.cloned.1.call-done), kind=kOutput, calls=%fused_computation.16 | convolution fusion | flops 1632632832 | bytes 20316160 | tf_op jit(solution)/shard_map/dot_general | solution.py:41
  475.8 0.0 copy-done.6
  475.8 2.6 convolution_convert_fusion.2
  478.5 0.0 all-reduce.2.cloned.1.call-update
  478.5 0.2 reduce-scatter.9.cloned.1.call-start
  478.7 31.1 %all-reduce.2.cloned.1.call-done = bf16[384,512]{1,0:T(8,128)(2,1)} async-done(((bf16[384,512]{1,0:T(8,128)(2,1)}), bf16[384,512]{1,0:T(8,128)(2,1)}) %all-reduce.2.cloned.1.call-update) | async-done | bytes 393232 | tf_op jit(solution)/shard_map/psum | solution.py:56
  509.8 4.1 fusion.18
  513.9 0.0 reduce-scatter.9.cloned.1.call-update
  513.9 0.0 reduce-scatter.11.cloned.1.call-start
  514.0 0.0 copy-done.2
  514.0 4.4 convolution_convert_fusion
  518.4 0.0 reduce-scatter.11.cloned.1.call-update
  518.5 0.0 reduce-scatter.5.cloned.1.call-start
  518.5 0.1 copy.38
  518.6 0.1 reshape.62
  518.7 3.3 copy.52
  522.0 0.0 copy-start
  522.0 25.2 %fusion.16 = f32[16,384,6,256]{3,1,2,0:T(8,128)} fusion(bf16[16,6,256,256]{3,2,1,0:T(8,128)(2,1)} %all-gather.8.cloned.1.call-done, bf16[384,16,256,1]{2,1,0,3:T(8,128)(2,1)S(1)} %bitcast.50), kind=kOutput, calls=%fused_computation.25 | convolution fusion | flops 4831838208 | bytes 53477376 | tf_op jit(solution)/shard_map/tjd,jkcd->tjkc/dot_general | solution.py:76
  547.2 0.0 copy-done
  547.2 5.9 broadcast_in_dim.19
  553.1 90.2 %scatter_fusion = f32[384,32,256]{2,0,1:T(8,128)} fusion(f32[384,32,256]{2,0,1:T(8,128)} %broadcast_in_dim.19, s32[96]{0:T(128)S(1)} %fusion.19, f32[96,384,256]{2,1,0:T(8,128)} %bitcast.46), kind=kCustom, calls=%fused_computation.1 | custom fusion | flops 9437184 | bytes 113246592 | tf_op jit(solution)/shard_map/scatter-add | solution.py:85
  643.3 5.4 convert_bitcast_fusion
  648.8 3.5 copy.51
  652.3 0.0 reduce-scatter.5.cloned.1.call-update
  652.3 0.3 reduce-scatter.7.cloned.1.call-start
  652.6 1.6 copy-done.1
  654.2 15.2 %fusion.6 = bf16[16,6,256,256]{3,2,1,0:T(8,128)(2,1)} fusion(bf16[16,6,384,256]{2,3,1,0:T(8,128)(2,1)} %copy.35, pred[16,6]{1,0:T(8,128)(4,1)S(1)} %copy.31, bf16[384,16,256,1]{2,1,0,3:T(8,128)(2,1)S(1)} %bitcast.51), kind=kOutput, calls=%fused_computation.10 | convolution fusion | flops 4847566848 | bytes 34603104 | tf_op jit(solution)/shard_map/tjkc,tjd->jkcd/dot_general | solution.py:70
  669.4 0.0 reduce-scatter.7.cloned.1.call-update
  669.5 0.0 reduce-scatter.9.cloned.1.call-done
  669.5 2.4 copy.42
  671.9 2.9 convert_element_type.59
  674.8 35.7 %reduce-scatter.5.cloned.1.call-done = bf16[384,2048]{1,0:T(8,128)(2,1)} async-done(((bf16[384,8192]{1,0:T(8,128)(2,1)}), bf16[384,2048]{1,0:T(8,128)(2,1)}) %reduce-scatter.5.cloned.1.call-update) | async-done | bytes 1572880 | tf_op jit(solution)/shard_map/reduce_scatter | solution.py:87
  710.4 4.1 convert_add_fusion
  714.5 210.0 %reduce-scatter.7.cloned.1.call-done = bf16[16,6,64,256]{3,2,1,0:T(8,128)(2,1)} async-done(((bf16[16,6,256,256]{3,2,1,0:T(8,128)(2,1)}), bf16[16,6,64,256]{3,2,1,0:T(8,128)(2,1)}) %reduce-scatter.7.cloned.1.call-update) | async-done | bytes 3145744 | tf_op jit(solution)/shard_map/reduce_scatter | solution.py:73
  924.5 5.5 convert_element_type.54
  (11 shorter events, 0.0 us)
Async XLA Ops:
  7.2 52.6 %copy-start.5 = (s32[64,6]{0,1:T(8,128)S(1)}, s32[64,6]{0,1:T(8,128)}, u32[]{:S(2)}) copy-start(s32[64,6]{0,1:T(8,128)} %param.7) | copy-start | bytes 4612
  7.2 51.4 %all-gather.10.cloned.1.call-start = ((), (), s32[]{:S(2)}) async-start(), calls=%async_computation.6 | async-start | bytes 2621440 | tf_op jit(solution)/shard_map/all_gather | solution.py:35
  7.9 97.4 %all-gather.6.cloned.1.call-start = ((), (), s32[]{:S(2)}) async-start(), calls=%async_computation.4 | async-start | bytes 7864320 | tf_op jit(solution)/shard_map/all_gather | solution.py:23
  10.6 154.6 %all-gather.12.cloned.1.call-start = ((), (), s32[]{:S(2)}) async-start(), calls=%async_computation.7 | async-start | bytes 10485760 | tf_op jit(solution)/shard_map/all_gather | solution.py:36
  58.6 326.3 %all-gather.8.cloned.1.call-start = ((), (), s32[]{:S(2)}) async-start(), calls=%async_computation.5 | async-start | bytes 15728640 | tf_op jit(solution)/shard_map/all_gather | solution.py:32
  59.1 406.1 %all-gather.14.cloned.1.call-start = ((), (), s32[]{:S(2)}) async-start(), calls=%async_computation.8 | async-start | bytes 5242880 | tf_op jit(solution)/shard_map/all_gather | solution.py:43
  59.7 450.0 %all-reduce.2.cloned.1.call-start = ((), (), s32[]{:S(2)}) async-start(), calls=%async_computation.10 | async-start | bytes 786432 | tf_op jit(solution)/shard_map/psum | solution.py:56
  465.3 10.5 %copy-start.6 = (bf16[512,4096]{1,0:T(8,128)(2,1)S(1)}, bf16[512,4096]{1,0:T(8,128)(2,1)}, u32[]{:S(2)}) copy-start(bf16[512,4096]{1,0:T(8,128)(2,1)} %all-gather.14.cloned.1.call-done) | copy-start | bytes 12582916
  475.8 38.2 %copy-start.2 = (bf16[384,4096]{1,0:T(8,128)(2,1)}, bf16[384,4096]{1,0:T(8,128)(2,1)S(1)}, u32[]{:S(2)}) copy-start(bf16[384,4096]{1,0:T(8,128)(2,1)S(1)} %get-tuple-element.22) | copy-start | bytes 9437188
  478.5 191.0 %reduce-scatter.9.cloned.1.call-start = ((), (), s32[]{:S(2)}) async-start(), calls=%async_computation.12 | async-start | bytes 2621440 | tf_op jit(solution)/shard_map/reduce_scatter | solution.py:66
  513.9 157.9 %reduce-scatter.11.cloned.1.call-start = ((), (), s32[]{:S(2)}) async-start(), calls=%async_computation.13 | async-start | bytes 5242880 | tf_op jit(solution)/shard_map/reduce_scatter | solution.py:60
  518.5 192.0 %reduce-scatter.5.cloned.1.call-start = ((), (), s32[]{:S(2)}) async-start(), calls=%async_computation.9 | async-start | bytes 7864320 | tf_op jit(solution)/shard_map/reduce_scatter | solution.py:87
  522.0 25.2 %copy-start = (bf16[48,8,16,256]{3,2,1,0:T(8,128)(2,1)}, bf16[48,8,16,256]{3,2,1,0:T(8,128)(2,1)S(1)}, u32[]{:S(2)}) copy-start(bf16[48,8,16,256]{3,2,1,0:T(8,128)(2,1)S(1)} %copy.52) | copy-start | bytes 9437188
  652.3 1.9 copy-start.1
  652.3 272.2 %reduce-scatter.7.cloned.1.call-start = ((), (), s32[]{:S(2)}) async-start(), calls=%async_computation.11 | async-start | bytes 15728640 | tf_op jit(solution)/shard_map/reduce_scatter | solution.py:73
  669.4 41.0 %copy-start.3 = (bf16[2048,512]{1,0:T(8,128)(2,1)S(1)}, bf16[2048,512]{1,0:T(8,128)(2,1)}, u32[]{:S(2)}) copy-start(bf16[2048,512]{1,0:T(8,128)(2,1)} %all-gather.10.cloned.1.call-done) | copy-start | bytes 6291460
  669.4 41.0 %copy-start.4 = (bf16[384,512]{1,0:T(8,128)(2,1)S(1)}, bf16[384,512]{1,0:T(8,128)(2,1)}, u32[]{:S(2)}) copy-start(bf16[384,512]{1,0:T(8,128)(2,1)} %all-reduce.2.cloned.1.call-done) | copy-start | bytes 1179652
Sparse Core Ops, SparseCore 0:
  9.6 48.9 all-gather.9
  60.7 44.5 all-gather.5
  106.9 58.2 all-gather.11
  166.6 218.2 all-gather.7
  386.3 78.9 all-gather.13
  478.6 31.1 all-reduce.1
  514.0 43.8 reduce-scatter.8
  560.2 76.0 reduce-scatter.10
  652.4 57.9 reduce-scatter.4
  712.6 211.8 reduce-scatter.6
where the time goes:
time: 939 us; the launch traced here: 937 us
  waiting for transfers between devices  654 us (70%)
  other arithmetic  104 us (11%)
  matrix products  91.5 us (10%)
  local copies, waits for them, and re-layouts  72.6 us (8%)
  between operations  14.3 us (2%)
    all_gather x1, waiting for transfers between devices, per_device(): lax.all_gather(blocks, 'dp', axis=2, tiled=True)  211 us
    reduce_scatter x1, waiting for transfers between devices, per_device(): lax.psum_scatter(block_term.astype(jnp.bfloat16), 'dp', scatter_dimension...  210 us
    scatter-add x1, other arithmetic, per_device(): placed = jnp.zeros((tok_rows, block_count, block_size), jnp.float32).at[:...  90.2 us
    all_gather x1, waiting for transfers between devices, per_device(): lax.all_gather(right_factor, 'dp', axis=0, tiled=True)  57.2 us
    all_gather x1, waiting for transfers between devices, per_device(): left_rows = lax.all_gather(left_factor, 'dp', axis=1, tiled=True)  47.9 us
    all_gather x1, waiting for transfers between devices, per_device(): full_tokens = lax.all_gather(tokens, 'tensor', axis=1, tiled=True)  45.2 us
    gather x2, local copies, waits for them, and re-layouts, per_device(): jnp.take(full_tokens.reshape(tok_rows, block_count, block_size), local_pa...  37.6 us
    reduce_scatter x1, waiting for transfers between devices, per_device(): lax.psum_scatter(placed.reshape(tok_rows, -1).astype(jnp.bfloat16), 'tens...  35.7 us
  transfers between devices with their start and end apart: 10, of which 8 were waited for; matrix products, arithmetic and copies ran while one was open for 26% of the time, Pallas kernels for 0%

commit v1 on v0

--- a/solution.py
+++ b/solution.py
@@ -5,6 +5,22 @@
 
 SQRT_HALF = 0.7071067811865476
 INV_ROOT_TWO_PI = 0.3989422804014327
+
+
+def summed_both_ways(x, axis, dim, term):
+    devices, index, rows = (lax.axis_size(axis), lax.axis_index(axis), x.shape[dim])
+    ahead = [(i, (i + 1) % devices) for i in range(devices)]
+    backward = [(i, (i - 1) % devices) for i in range(devices)]
+    middle = devices // 2
+    from_left = from_right = x
+    total = term(x, index * rows)
+    for step in range(1, middle + 1):
+        from_left = lax.ppermute(from_left, axis, ahead)
+        if step < devices - middle:
+            from_right = lax.ppermute(from_right, axis, backward)
+            total = total + term(from_right, (index + step) % devices * rows)
+        total = total + term(from_left, (index - step) % devices * rows)
+    return total
 
 
 def gelu_parts(preact):
@@ -26,11 +42,16 @@
     local_pattern = lax.dynamic_slice_in_dim(pattern, tensor_rank * local_cols, local_cols, 0)
     picked = jnp.take(full_tokens.reshape(tok_rows, block_count, block_size), local_pattern, axis=1)
     inputs = picked
-    butterfly = jnp.einsum(
-        "tjkc,jkcd->tjd",
-        inputs,
-        lax.all_gather(blocks, "dp", axis=2, tiled=True),
-        preferred_element_type=jnp.float32,
+    butterfly = summed_both_ways(
+        blocks,
+        "dp",
+        2,
+        lambda own_block, start: jnp.einsum(
+            "tjkc,jkcd->tjd",
+            lax.dynamic_slice_in_dim(inputs, start, own_block.shape[2], axis=3),
+            own_block,
+            preferred_element_type=jnp.float32,
+        ),
     )
     left_rows = lax.all_gather(left_factor, "dp", axis=1, tiled=True)
     whole_left = lax.all_gather(left_rows, "tensor", axis=0, tiled=True)

time: 939 us -> 1040 us (1.11)
  waiting for transfers between devices: 654 us -> 730 us
  other arithmetic: 104 us -> 118 us
    ppermute x0 -> x3, waiting for transfers between devices: none -> 192 us  [the longest x2 142 us: summed_both_ways(): from_left = lax.ppermute(from_left, axis, ahead)]
    all_gather x1, waiting for transfers between devices: 57.2 us -> 0.02 us  [per_device(): lax.all_gather(right_factor, 'dp', axis=0, tiled=True)]
    all_gather x1, waiting for transfers between devices: 45.2 us -> 0.01 us  [per_device(): full_tokens = lax.all_gather(tokens, 'tensor', axis=1, tiled=True)]
    dot_general x1 -> x4, matrix products: 16.6 us -> 34.8 us  [per_device(): jnp.einsum('tjkc,jkcd->tjd', lax.dynamic_slice_in_dim(inputs, start, own_...]
    all_gather x1, waiting for transfers between devices: 13.6 us -> 0.01 us  [per_device(): whole_left = lax.all_gather(left_rows, 'tensor', axis=0, tiled=True)]
  transfers between devices with their start and end apart: 10 -> 13, of which waited for: 8 -> 8; matrix products, arithmetic and copies ran while one was open for 26% -> 26% of each run, Pallas kernels for 0% -> 0%
where the time goes in v1:
time: 1040 us
  waiting for transfers between devices  730 us (70%)
  other arithmetic  118 us (11%)
  matrix products  96.8 us (9%)
  local copies, waits for them, and re-layouts  72.4 us (7%)
  between operations  14.3 us (1%)
    reduce_scatter x1, waiting for transfers between devices, per_device(): lax.psum_scatter(block_term.astype(jnp.bfloat16), 'dp', scatter_dimension...  210 us
    all_gather x1, waiting for transfers between devices, per_device(): lax.all_gather(blocks, 'dp', axis=2, tiled=True)  208 us
    ppermute x2, waiting for transfers between devices, summed_both_ways(): from_left = lax.ppermute(from_left, axis, ahead)  142 us
    scatter-add x1, other arithmetic, per_device(): placed = jnp.zeros((tok_rows, block_count, block_size), jnp.float32).at[:...  90.1 us
    ppermute x1, waiting for transfers between devices, summed_both_ways(): from_right = lax.ppermute(from_right, axis, backward)  50.4 us
    all_gather x1, waiting for transfers between devices, per_device(): left_rows = lax.all_gather(left_factor, 'dp', axis=1, tiled=True)  47.8 us
    reduce_scatter x1, waiting for transfers between devices, per_device(): lax.psum_scatter(placed.reshape(tok_rows, -1).astype(jnp.bfloat16), 'tens...  39.3 us
    gather x2, local copies, waits for them, and re-layouts, per_device(): jnp.take(full_tokens.reshape(tok_rows, block_count, block_size), local_pa...  36.7 us
  transfers between devices with their start and end apart: 13, of which 8 were waited for; matrix products, arithmetic and copies ran while one was open for 26% of the time, Pallas kernels for 0%

profile of v1, /device:TPU:0, one launch (start us, length us, event | category | flops | bytes accessed | tf_op | source)
XLA Modules:
  0.0 1036.4 jit_solution(3268159570057184022)
XLA Ops:
  7.2 0.0 all-gather.8.cloned.1.call-start
  7.2 0.7 all-gather.8.cloned.1.call-update
  7.9 0.0 all-gather.6.cloned.1.call-start
  8.0 2.7 copy.29
  10.7 0.0 all-gather.6.cloned.1.call-update
  10.7 0.0 all-gather.10.cloned.1.call-start
  10.8 47.8 %all-gather.8.cloned.1.call-done = bf16[2048,512]{1,0:T(8,128)(2,1)} async-done(((bf16[2048,128]{1,0:T(8,128)(2,1)}), bf16[2048,512]{1,0:T(8,128)(2,1)}) %all-gather.8.cloned.1.call-update) | async-done | bytes 2097168 | tf_op jit(solution)/shard_map/all_gather | solution.py:56
  58.6 0.0 all-gather.10.cloned.1.call-update
  58.6 0.0 all-gather.12.cloned.1.call-start
  58.6 0.2 collective-permute-start.1
  58.9 0.3 all-gather.12.cloned.1.call-update
  59.2 0.0 all-reduce.2.cloned.1.call-start
  59.2 3.4 collective-permute-start
  62.6 0.1 compare_and_fusion
  62.7 0.1 copy.28
  62.8 0.1 copy.30
  62.9 0.1 reshape.67
  63.0 68.6 %collective-permute-done.1 = bf16[16,6,64,256]{3,2,1,0:T(8,128)(2,1)} collective-permute-done((bf16[16,6,64,256]{3,2,1,0:T(8,128)(2,1)S(1)}, bf16[16,6,64,256]{3,2,1,0:T(8,128)(2,1)}, u32[]{:S(2)}, u32[]{:S(2)}) %collective-permute-start.1) | collective-permute-done | bytes 3145760 | tf_op jit(solution)/shard_map/ppermute | solution.py:18
  131.6 8.6 copy.31
  140.2 12.0 %gather_fusion = bf16[96,384,256]{2,1,0:T(8,128)(2,1)} fusion(bf16[384,32,256]{2,0,1:T(8,128)(2,1)} %copy.31, s32[1024]{0:T(1024)S(1)} %pad_clamp_fusion), kind=kCustom, calls=%fused_computation | custom fusion | bytes 37749120 | tf_op jit(solution)/shard_map/jit(_take)/gather | solution.py:43
  152.2 24.7 %copy.32 = bf16[96,384,256]{1,2,0:T(8,128)(2,1)} copy(bf16[96,384,256]{2,1,0:T(8,128)(2,1)} %gather_fusion) | data formatting | bytes 37748736 | tf_op jit(solution)/shard_map/jit(_take)/gather | solution.py:43
  177.0 10.3 broadcast_select_fusion
  187.3 5.3 fusion.17
  192.6 9.1 fusion.13
  201.7 50.4 %collective-permute-done = bf16[16,6,64,256]{3,2,1,0:T(8,128)(2,1)} collective-permute-done((bf16[16,6,64,256]{3,2,1,0:T(8,128)(2,1)S(1)}, bf16[16,6,64,256]{3,2,1,0:T(8,128)(2,1)}, u32[]{:S(2)}, u32[]{:S(2)}) %collective-permute-start) | collective-permute-done | bytes 3145760 | tf_op jit(solution)/shard_map/ppermute | solution.py:20
  252.1 6.7 fusion.15
  258.8 73.2 %collective-permute-done.2 = bf16[16,6,64,256]{3,2,1,0:T(8,128)(2,1)} collective-permute-done((bf16[16,6,64,256]{3,2,1,0:T(8,128)(2,1)}, bf16[16,6,64,256]{3,2,1,0:T(8,128)(2,1)}, u32[]{:S(2)}, u32[]{:S(2)}) %collective-permute-start.2) | collective-permute-done | bytes 3145760 | tf_op jit(solution)/shard_map/ppermute | solution.py:18
  332.0 13.6 %bitcast_add_fusion = f32[16,384,256]{1,2,0:T(8,128)} fusion(f32[16,384,256,1]{1,2,3,0:T(8,128)} %fusion.13, f32[16,384,256,1]{1,2,3,0:T(8,128)} %fusion.15, f32[16,384,256,1]{1,2,3,0:T(8,128)} %fusion.17, bf16[16,6,64,256]{3,2,1,0:T(8,128)(2,1)} %collective-permute-done.2, bf16[16,6,384,256]{2,3,1,0:T(8,128)(2,1)} %copy-done, s32[]{:T(128)S(6)} %select_n.58), kind=kOutput, calls=%fused_computation.13 | convolution fusion | flops 1212678144 | bytes 33030148 | tf_op jit(solution)/shard_map/tjkc,jkcd->tjd/dot_general | solution.py:49
  345.7 6.6 copy.33
  352.3 8.6 convolution_convert_fusion.3
  361.0 0.0 all-gather.12.cloned.1.call-done
  361.0 4.1 fusion.34
  365.2 0.8 copy-done.6
  366.0 4.2 fusion.10
  370.2 2.6 convolution_convert_fusion.2
  372.8 0.0 all-gather.14.cloned.1.call-start
  372.8 0.5 all-gather.14.cloned.1.call-update
  373.4 0.0 reduce-scatter.9.cloned.1.call-start
  373.4 31.2 %all-reduce.2.cloned.1.call-done = bf16[384,512]{1,0:T(8,128)(2,1)} async-done(((bf16[384,512]{1,0:T(8,128)(2,1)}), bf16[384,512]{1,0:T(8,128)(2,1)}) %all-reduce.2.cloned.1.call-update) | async-done | bytes 393232 | tf_op jit(solution)/shard_map/psum | solution.py:77
  404.6 4.1 fusion.26
  408.8 0.0 reduce-scatter.11.cloned.1.call-start
  408.8 4.4 convolution_convert_fusion
  413.2 0.0 reduce-scatter.11.cloned.1.call-update
  413.2 0.0 reduce-scatter.5.cloned.1.call-start
  413.3 0.1 copy.34
  413.4 0.1 reshape.62
  413.5 2.8 copy.50
  416.2 208.2 %all-gather.14.cloned.1.call-done = bf16[16,6,256,256]{3,2,1,0:T(8,128)(2,1)} async-done(((bf16[16,6,64,256]{3,2,1,0:T(8,128)(2,1)}), bf16[16,6,256,256]{3,2,1,0:T(8,128)(2,1)}) %all-gather.14.cloned.1.call-update) | async-done | bytes 12582928 | tf_op jit(solution)/shard_map/all_gather | solution.py:100
  624.4 20.3 %fusion.24 = f32[16,384,6,256]{3,1,2,0:T(8,128)} fusion(bf16[16,6,256,256]{3,2,1,0:T(8,128)(2,1)} %all-gather.14.cloned.1.call-done, bf16[384,16,256,1]{2,1,0,3:T(8,128)(2,1)} %bitcast.80), kind=kOutput, calls=%fused_computation.35 | convolution fusion | flops 4831838208 | bytes 53477376 | tf_op jit(solution)/shard_map/tjd,jkcd->tjkc/dot_general | solution.py:97
  644.7 6.0 broadcast_in_dim.19
  650.7 90.1 %scatter_fusion = f32[384,32,256]{2,0,1:T(8,128)} fusion(f32[384,32,256]{2,0,1:T(8,128)} %broadcast_in_dim.19, s32[96]{0:T(128)S(1)} %fusion.33, f32[96,384,256]{2,1,0:T(8,128)} %bitcast.74), kind=kCustom, calls=%fused_computation.1 | custom fusion | flops 9437184 | bytes 113246592 | tf_op jit(solution)/shard_map/scatter-add | solution.py:106
  740.8 5.5 convert_bitcast_fusion
  746.3 3.5 copy.49
  749.8 0.0 reduce-scatter.7.cloned.1.call-start
  749.9 1.8 copy-done.2
  751.7 13.8 %fusion.2 = bf16[16,6,256,256]{3,2,1,0:T(8,128)(2,1)} fusion(bf16[16,6,384,256]{2,3,1,0:T(8,128)(2,1)} %copy-done, bf16[384,16,256,1]{2,1,0,3:T(8,128)(2,1)S(1)} %bitcast.81), kind=kOutput, calls=%fused_computation.6 | convolution fusion | flops 4838129664 | bytes 34603008 | tf_op jit(solution)/shard_map/tjkc,tjd->jkcd/dot_general | solution.py:91
  765.5 0.0 reduce-scatter.7.cloned.1.call-update
  765.5 0.0 reduce-scatter.9.cloned.1.call-done
  765.6 2.4 copy.38
  767.9 2.8 convert_element_type.59
  770.7 39.3 %reduce-scatter.5.cloned.1.call-done = bf16[384,2048]{1,0:T(8,128)(2,1)} async-done(((bf16[384,8192]{1,0:T(8,128)(2,1)}), bf16[384,2048]{1,0:T(8,128)(2,1)}) %reduce-scatter.5.cloned.1.call-update) | async-done | bytes 1572880 | tf_op jit(solution)/shard_map/reduce_scatter | solution.py:108
  810.0 4.1 convert_add_fusion
  814.1 210.0 %reduce-scatter.7.cloned.1.call-done = bf16[16,6,64,256]{3,2,1,0:T(8,128)(2,1)} async-done(((bf16[16,6,256,256]{3,2,1,0:T(8,128)(2,1)}), bf16[16,6,64,256]{3,2,1,0:T(8,128)(2,1)}) %reduce-scatter.7.cloned.1.call-update) | async-done | bytes 3145744 | tf_op jit(solution)/shard_map/reduce_scatter | solution.py:94
  1024.1 5.5 convert_element_type.54
  (26 shorter events, 0.1 us)
Async XLA Ops:
  7.2 51.5 %copy-start.3 = (bf16[16,6,64,256]{3,2,1,0:T(8,128)(2,1)S(1)}, bf16[16,6,64,256]{3,2,1,0:T(8,128)(2,1)}, u32[]{:S(2)}) copy-start(bf16[16,6,64,256]{3,2,1,0:T(8,128)(2,1)} %param.8) | copy-start | bytes 9437188
  7.2 55.5 %copy-start.8 = (s32[64,6]{0,1:T(8,128)S(1)}, s32[64,6]{0,1:T(8,128)}, u32[]{:S(2)}) copy-start(s32[64,6]{0,1:T(8,128)} %param.7) | copy-start | bytes 4612
  7.2 51.4 %all-gather.8.cloned.1.call-start = ((), (), s32[]{:S(2)}) async-start(), calls=%async_computation.5 | async-start | bytes 2621440 | tf_op jit(solution)/shard_map/all_gather | solution.py:56
  7.9 123.7 %all-gather.6.cloned.1.call-start = ((), (), s32[]{:S(2)}) async-start(), calls=%async_computation.4 | async-start | bytes 7864320 | tf_op jit(solution)/shard_map/all_gather | solution.py:39
  10.7 341.6 %all-gather.10.cloned.1.call-start = ((), (), s32[]{:S(2)}) async-start(), calls=%async_computation.6 | async-start | bytes 10485760 | tf_op jit(solution)/shard_map/all_gather | solution.py:57
  58.6 302.4 %all-gather.12.cloned.1.call-start = ((), (), s32[]{:S(2)}) async-start(), calls=%async_computation.7 | async-start | bytes 5242880 | tf_op jit(solution)/shard_map/all_gather | solution.py:64
  58.6 73.0 %collective-permute-start.1 = (bf16[16,6,64,256]{3,2,1,0:T(8,128)(2,1)S(1)}, bf16[16,6,64,256]{3,2,1,0:T(8,128)(2,1)}, u32[]{:S(2)}, u32[]{:S(2)}) collective-permute-start(bf16[16,6,64,256]{3,2,1,0:T(8,128)(2,1)S(1)} %copy-done.3), channel_id=1, source_target_pairs={{0,4},{4,8},{8,12},{12,0},{1,5},{5,9},{9,13},{13,1},{2,6},{6,10},{... | collective-permute-start | bytes 9437192 | tf_op jit(solution)/shard_map/ppermute | solution.py:18
  59.2 345.5 %all-reduce.2.cloned.1.call-start = ((), (), s32[]{:S(2)}) async-start(), calls=%async_computation.10 | async-start | bytes 786432 | tf_op jit(solution)/shard_map/psum | solution.py:77
  59.2 192.9 %collective-permute-start = (bf16[16,6,64,256]{3,2,1,0:T(8,128)(2,1)S(1)}, bf16[16,6,64,256]{3,2,1,0:T(8,128)(2,1)}, u32[]{:S(2)}, u32[]{:S(2)}) collective-permute-start(bf16[16,6,64,256]{3,2,1,0:T(8,128)(2,1)S(1)} %copy-done.3), channel_id=1, source_target_pairs={{0,12},{4,0},{8,4},{12,8},{1,13},{5,1},{9,5},{13,9},{2,14},{6,2},{... | collective-permute-start | bytes 9437192 | tf_op jit(solution)/shard_map/ppermute | solution.py:20
  131.6 200.4 %collective-permute-start.2 = (bf16[16,6,64,256]{3,2,1,0:T(8,128)(2,1)}, bf16[16,6,64,256]{3,2,1,0:T(8,128)(2,1)}, u32[]{:S(2)}, u32[]{:S(2)}) collective-permute-start(bf16[16,6,64,256]{3,2,1,0:T(8,128)(2,1)} %collective-permute-done.1), channel_id=1, source_target_pairs={{0,4},{4,8},{8,12},{12,0},{1,5},{5,9},{9,13},{13,1},{2,6},{6,10},{... | collective-permute-start | bytes 9437192 | tf_op jit(solution)/shard_map/ppermute | solution.py:18
  187.3 64.8 %copy-start = (bf16[16,6,384,256]{2,3,1,0:T(8,128)(2,1)}, bf16[16,6,384,256]{2,3,1,0:T(8,128)(2,1)S(1)}, u32[]{:S(2)}) copy-start(bf16[16,6,384,256]{2,3,1,0:T(8,128)(2,1)S(1)} %broadcast_select_fusion) | copy-start | bytes 56623108
  361.0 4.2 copy-start.1
  361.0 5.0 copy-start.6
  366.0 4.2 copy-start.5
  372.8 251.6 %all-gather.14.cloned.1.call-start = ((), (), s32[]{:S(2)}) async-start(), calls=%async_computation.8 | async-start | bytes 15728640 | tf_op jit(solution)/shard_map/all_gather | solution.py:100
  373.4 392.2 %reduce-scatter.9.cloned.1.call-start = ((), (), s32[]{:S(2)}) async-start(), calls=%async_computation.12 | async-start | bytes 2621440 | tf_op jit(solution)/shard_map/reduce_scatter | solution.py:87
  408.8 359.2 %reduce-scatter.11.cloned.1.call-start = ((), (), s32[]{:S(2)}) async-start(), calls=%async_computation.13 | async-start | bytes 5242880 | tf_op jit(solution)/shard_map/reduce_scatter | solution.py:81
  413.2 396.8 %reduce-scatter.5.cloned.1.call-start = ((), (), s32[]{:S(2)}) async-start(), calls=%async_computation.9 | async-start | bytes 7864320 | tf_op jit(solution)/shard_map/reduce_scatter | solution.py:108
  749.8 1.9 copy-start.2
  749.8 274.3 %reduce-scatter.7.cloned.1.call-start = ((), (), s32[]{:S(2)}) async-start(), calls=%async_computation.11 | async-start | bytes 15728640 | tf_op jit(solution)/shard_map/reduce_scatter | solution.py:94
  765.5 44.5 %copy-start.4 = (bf16[2048,512]{1,0:T(8,128)(2,1)S(1)}, bf16[2048,512]{1,0:T(8,128)(2,1)}, u32[]{:S(2)}) copy-start(bf16[2048,512]{1,0:T(8,128)(2,1)} %all-gather.8.cloned.1.call-done) | copy-start | bytes 6291460
  765.5 44.5 %copy-start.7 = (bf16[384,512]{1,0:T(8,128)(2,1)S(1)}, bf16[384,512]{1,0:T(8,128)(2,1)}, u32[]{:S(2)}) copy-start(bf16[384,512]{1,0:T(8,128)(2,1)} %all-reduce.2.cloned.1.call-done) | copy-start | bytes 1179652
Sparse Core Ops, SparseCore 0:
  9.6 48.9 all-gather.7
  60.7 44.5 all-gather.5
  106.9 58.2 all-gather.9
  166.6 145.8 all-gather.11
  372.9 31.6 all-reduce.1
  406.1 218.2 all-gather.13
  627.4 41.9 reduce-scatter.8
  671.7 76.0 reduce-scatter.10
  751.1 58.8 reduce-scatter.4
  812.2 211.8 reduce-scatter.6
